TPU v7x, 32 devices: a whole 2x2x4 slice. The times are simulated.
32 devices in a mesh: rep: 2 (over x), seq: 4 (over y, core), dp: 4 (over z).
Axes of the slice: x: 2, y: 2, z: 4, core: 2. Of those that a mesh axis runs over, the one named last changes fastest.
Arguments:
- queries: bfloat16 [8, 1024, 2048], P(('rep', 'dp'), 'seq'), parts along dimension 0, may hold values from -20 to 20
- keys: bfloat16 [8, 1024, 2048], P(('rep', 'dp'), 'seq'), parts along dimension 0, may hold values from -20 to 20
- values: bfloat16 [8, 1024, 2048], P(('rep', 'dp'), 'seq'), parts along dimension 0, may hold values from -6 to 6
- lengths: int32 [8, 8], P(('rep', 'dp')), parts along dimension 0, may hold values from 1 to 512, 1024 in all within a row
Outputs:
- attended: bfloat16 [8, 1024, 2048], P(('rep', 'dp'), 'seq'), parts along dimension 0
- doc_vectors: float32 [8, 8, 2048], P(('rep', 'dp')), parts along dimension 0
There are 2 independent parts, one for each index of `rep`. A program takes and returns all parts, laid end to end along the dimension named above; each array names one. Nothing has to cross between parts.
Inputs may be any that keep to these rules, and one draw needn't show every extreme that they name: Each row holds 8 lengths that sum to 1024, and its largest is 512.
All inputs are finite; a program needn't handle non-finite values.
Results may differ from a plain program's by a relative error of at most 0.0051.
Values may be sent and summed in bfloat16 or wider, within the bound.
A program may use at most 64 MiB of HBM per device.

v0:
```python
import jax
import jax.numpy as jnp
from jax import lax
from jax.sharding import PartitionSpec as P

HEADS = 16
HD = 128


def doc_index(lens, positions):
    ends = jnp.cumsum(lens)
    return jnp.sum((ends[None, :] <= positions[:, None]).astype(jnp.int32), axis=1)


def attend(queries_h, keys_h, values_h, doc_ids):
    stream = queries_h.shape[0]
    block = 512
    count = stream // block
    scale = 1.0 / queries_h.shape[2] ** 0.5

    def one_block(index):
        start = index * block
        q_block = lax.dynamic_slice_in_dim(queries_h, start, block, 0)
        ids = lax.dynamic_slice_in_dim(doc_ids, start, block, 0)
        scores = (
            jnp.einsum("qhd,khd->hqk", q_block, keys_h, preferred_element_type=jnp.float32) * scale
        )
        same = ids[:, None] == doc_ids[None, :]
        scores = jnp.where(same[None], scores, -1e30)
        top = jnp.max(scores, axis=2, keepdims=True)
        expo = jnp.exp(scores - top)
        probs = expo / jnp.sum(expo, axis=2, keepdims=True)
        weights = probs.astype(jnp.bfloat16)
        mixed = jnp.einsum("hqk,khd->qhd", weights, values_h, preferred_element_type=jnp.float32)
        return mixed.astype(jnp.bfloat16)

    out = lax.map(one_block, jnp.arange(count, dtype=jnp.int32))
    return out.reshape(stream, queries_h.shape[1], queries_h.shape[2])


def normalize(sums):
    return sums / jnp.sqrt(jnp.mean(sums * sums, axis=-1, keepdims=True) + 1e-06)


def per_device(queries, keys, values, lengths):
    members = lax.axis_size("seq")
    tok_rows = queries.shape[1]
    width = queries.shape[2]
    local_heads = HEADS // members
    group_width = local_heads * HD
    stream = tok_rows * members
    lens = lengths[0]
    doc_count = lens.shape[0]
    q_split = queries[0].reshape(tok_rows, members, group_width)
    k_split = keys[0].reshape(tok_rows, members, group_width)
    v_split = values[0].reshape(tok_rows, members, group_width)
    q_heads, k_heads, v_heads = (
        lax.all_to_all(q_split, "seq", split_axis=1, concat_axis=0, tiled=True),
        lax.all_to_all(k_split, "seq", split_axis=1, concat_axis=0, tiled=True),
        lax.all_to_all(v_split, "seq", split_axis=1, concat_axis=0, tiled=True),
    )
    all_ids = doc_index(lens, jnp.arange(stream, dtype=jnp.int32))
    head_out = attend(
        q_heads.reshape(stream, local_heads, HD),
        k_heads.reshape(stream, local_heads, HD),
        v_heads.reshape(stream, local_heads, HD),
        all_ids,
    )
    head_rows = head_out.reshape(stream, 1, group_width)
    back = lax.all_to_all(head_rows, "seq", split_axis=0, concat_axis=1, tiled=True)
    rows = back.reshape(tok_rows, width)
    doc_range = jnp.arange(doc_count, dtype=jnp.int32)
    start = lax.axis_index("seq") * tok_rows
    local_ids = doc_index(lens, start + jnp.arange(tok_rows, dtype=jnp.int32))
    onehot_local = (local_ids[None, :] == doc_range[:, None]).astype(jnp.bfloat16)
    token_part = jnp.dot(onehot_local, rows, preferred_element_type=jnp.float32)
    sums = lax.psum(token_part, "seq")
    return (rows.reshape(1, tok_rows, width), normalize(sums).reshape(1, doc_count, width))


def solution(mesh):
    return jax.shard_map(
        per_device,
        mesh=mesh,
        in_specs=(
            P(("rep", "dp"), "seq", None),
            P(("rep", "dp"), "seq", None),
            P(("rep", "dp"), "seq", None),
            P(("rep", "dp"), None),
        ),
        out_specs=(P(("rep", "dp"), "seq", None), P(("rep", "dp"), None, None)),
        check_vma=False,
    )
```

profile of v0, /device:TPU:0, one launch (start us, length us, event | category | flops | bytes accessed | tf_op | source)
XLA Modules:
  0.0 174.2 jit_solution(7149144636139171197)
XLA Ops:
  7.2 1.8 %reshape_squeeze.10 = bf16[256,4,512]{2,1,0:T(4,128)(2,1)S(1)} reshape(bf16[1,256,2048]{2,1,0:T(8,128)(2,1)} %param.7) | data formatting | bytes 2097152 | tf_op jit(solution)/shard_map/reshape;squeeze | solution.py:55
  9.0 1.2 copy.35
  10.2 4.2 %all-to-all-start.1 = ((bf16[256,4,512]{2,0,1:T(8,128)(2,1)}), bf16[256,4,512]{2,0,1:T(8,128)(2,1)S(1)}, u32[]{:S(2)}, u32[]{:S(2)}) async-start(bf16[256,4,512]{2,0,1:T(8,128)(2,1)} %copy.35), calls=%async_computation.1 | async-start | bytes 2097152 | tf_op jit(solution)/shard_map/all_to_all | solution.py:59
  14.4 1.8 %reshape_squeeze.11 = bf16[256,4,512]{2,1,0:T(4,128)(2,1)S(1)} reshape(bf16[1,256,2048]{2,1,0:T(8,128)(2,1)} %param.8) | data formatting | bytes 2097152 | tf_op jit(solution)/shard_map/reshape;squeeze | solution.py:56
  16.3 1.2 copy.36
  17.5 11.4 %all-to-all-done.1 = bf16[256,4,512]{2,0,1:T(8,128)(2,1)S(1)} async-done(((bf16[256,4,512]{2,0,1:T(8,128)(2,1)}), bf16[256,4,512]{2,0,1:T(8,128)(2,1)S(1)}, u32[]{:S(2)}, u32[]{:S(2)}) %all-to-all-start.1) | async-done | bytes 1048608 | tf_op jit(solution)/shard_map/all_to_all | solution.py:59
  28.9 3.5 %all-to-all-start.2 = ((bf16[256,4,512]{2,0,1:T(8,128)(2,1)}), bf16[256,4,512]{2,0,1:T(8,128)(2,1)S(1)}, u32[]{:S(2)}, u32[]{:S(2)}) async-start(bf16[256,4,512]{2,0,1:T(8,128)(2,1)} %copy.36), calls=%async_computation.2 | async-start | bytes 2097152 | tf_op jit(solution)/shard_map/all_to_all | solution.py:60
  32.4 1.8 %reshape_squeeze.9 = bf16[256,4,512]{2,1,0:T(4,128)(2,1)S(1)} reshape(bf16[1,256,2048]{2,1,0:T(8,128)(2,1)} %param.6) | data formatting | bytes 2097152 | tf_op jit(solution)/shard_map/reshape;squeeze | solution.py:54
  34.3 1.2 copy.34
  35.5 11.4 %all-to-all-done.2 = bf16[256,4,512]{2,0,1:T(8,128)(2,1)S(1)} async-done(((bf16[256,4,512]{2,0,1:T(8,128)(2,1)}), bf16[256,4,512]{2,0,1:T(8,128)(2,1)S(1)}, u32[]{:S(2)}, u32[]{:S(2)}) %all-to-all-start.2) | async-done | bytes 1048608 | tf_op jit(solution)/shard_map/all_to_all | solution.py:60
  46.9 3.5 %all-to-all-start = ((bf16[256,4,512]{2,0,1:T(8,128)(2,1)}), bf16[256,4,512]{2,0,1:T(8,128)(2,1)S(1)}, u32[]{:S(2)}, u32[]{:S(2)}) async-start(bf16[256,4,512]{2,0,1:T(8,128)(2,1)} %copy.34), calls=%async_computation | async-start | bytes 2097152 | tf_op jit(solution)/shard_map/all_to_all | solution.py:58
  50.7 1.2 reshape.95
  51.8 2.4 %copy.38 = bf16[1024,4,128]{2,0,1:T(8,128)(2,1)} copy(bf16[1024,4,128]{2,1,0:T(4,128)(2,1)} %reshape.95) | data formatting | bytes 2097152 | tf_op jit(solution)/shard_map/while | solution.py:37
  54.5 1.1 copy.39
  55.7 9.1 %all-to-all-done = bf16[256,4,512]{2,0,1:T(8,128)(2,1)S(1)} async-done(((bf16[256,4,512]{2,0,1:T(8,128)(2,1)}), bf16[256,4,512]{2,0,1:T(8,128)(2,1)S(1)}, u32[]{:S(2)}, u32[]{:S(2)}) %all-to-all-start) | async-done | bytes 1048608 | tf_op jit(solution)/shard_map/all_to_all | solution.py:58
  65.1 31.1 %while.10 = (s32[]{:T(128)}, bf16[2,512,4,128]{3,2,1,0:T(4,128)(2,1)}, s32[2]{0:T(128)S(1)}, s32[1024]{0:T(1024)S(1)}, bf16[1024,4,128]{2,1,0:T(4,128)(2,1)S(1)}...) while((s32[]{:T(128)}, ...), condition=%wide.region_5.6_spmd, body=%wide.region_2.5_spmd.sunk | while | flops 1087112192 | bytes 27290316 | solution.py:37
  67.1 7.6 %fusion.38 = (f32[4,512]{1,0:T(4,128)S(1)}, f32[4,512,1024]{2,1,0:T(8,128)}) fusion(pred[512,1024]{1,0:T(8,128)(4,1)S(1)} %broadcast_compare_fusion.2, bf16[1024,4,128]{2,0,1:T(8,128)(2,1)} %get-tuple-element.164, bf16[512,4,128]{2,1,0:T(4,128)(2,1)S(1)} %constant_dynamic-slice_fusion.2), kind=kOutput, calls=%fused_computation.30.clone.1 | convolution fusion | flops 545260544 | bytes 10493952 | tf_op jit(solution)/shard_map/while/body/eval_jaxpr/sub | solution.py:31
  74.7 4.7 %fusion.39 = bf16[1,512,4,128]{3,1,2,0:T(8,128)(2,1)S(1)} fusion(bf16[1024,4,128]{2,0,1:T(8,128)(2,1)S(1)} %copy-done, f32[4,512,1024]{2,1,0:T(8,128)} %get-tuple-element.135, f32[4,512]{1,0:T(4,128)S(1)} %get-tuple-element.136), kind=kOutput, calls=%fused_computation.10.clone.1 | convolution fusion | flops 541327360 | bytes 9969664 | tf_op jit(solution)/shard_map/while/body/eval_jaxpr/hqk,khd->qhd/dot_general | solution.py:34
  79.4 1.2 copy_dynamic-update-slice_fusion.2
  82.7 7.6 %fusion.38 = (f32[4,512]{1,0:T(4,128)S(1)}, f32[4,512,1024]{2,1,0:T(8,128)}) fusion(pred[512,1024]{1,0:T(8,128)(4,1)S(1)} %broadcast_compare_fusion.2, bf16[1024,4,128]{2,0,1:T(8,128)(2,1)} %get-tuple-element.164, bf16[512,4,128]{2,1,0:T(4,128)(2,1)S(1)} %constant_dynamic-slice_fusion.2), kind=kOutput, calls=%fused_computation.30.clone.1 | convolution fusion | flops 545260544 | bytes 10493952 | tf_op jit(solution)/shard_map/while/body/eval_jaxpr/sub | solution.py:31
  90.3 4.7 %fusion.39 = bf16[1,512,4,128]{3,1,2,0:T(8,128)(2,1)S(1)} fusion(bf16[1024,4,128]{2,0,1:T(8,128)(2,1)S(1)} %copy-done, f32[4,512,1024]{2,1,0:T(8,128)} %get-tuple-element.135, f32[4,512]{1,0:T(4,128)S(1)} %get-tuple-element.136), kind=kOutput, calls=%fused_computation.10.clone.1 | convolution fusion | flops 541327360 | bytes 9969664 | tf_op jit(solution)/shard_map/while/body/eval_jaxpr/hqk,khd->qhd/dot_general | solution.py:34
  95.0 1.2 copy_dynamic-update-slice_fusion.2
  96.2 6.0 %reshape_reshape.8 = bf16[1024,1,512]{2,1,0:T(2,128)(2,1)S(1)} reshape(bf16[2,512,4,128]{3,2,1,0:T(4,128)(2,1)} %get-tuple-element.39) | data formatting | bytes 2097152 | tf_op jit(solution)/shard_map/reshape;reshape | solution.py:69
  102.7 7.0 %reduce = bf16[1024,512]{1,0:T(8,128)(2,1)S(1)} reduce(bf16[1024,1,512]{2,1,0:T(2,128)(2,1)S(1)} %reshape_reshape.8, bf16[]{:T(256)} %broadcast.57), dimensions={1}, to_apply=%reshape_reshape.8.reduce_sub_computation | reduce | bytes 2097154 | tf_op jit(solution)/shard_map/reshape;reshape | solution.py:69
  109.8 2.0 %reshape.99 = bf16[4,2,65536]{2,1,0:T(2,128)(2,1)} reshape(bf16[1024,512]{1,0:T(8,128)(2,1)S(1)} %reduce) | data formatting | bytes 2097152
  111.8 3.5 %all-to-all-start.3 = ((bf16[4,2,65536]{2,1,0:T(2,128)(2,1)}), bf16[4,2,65536]{2,1,0:T(2,128)(2,1)S(1)}, u32[]{:S(2)}, u32[]{:S(2)}) async-start(bf16[4,2,65536]{2,1,0:T(2,128)(2,1)} %reshape.99), calls=%async_computation.3 | async-start | bytes 2097152 | tf_op jit(solution)/shard_map/all_to_all | solution.py:70
  115.5 14.3 %all-to-all-done.3 = bf16[4,2,65536]{2,1,0:T(2,128)(2,1)S(1)} async-done(((bf16[4,2,65536]{2,1,0:T(2,128)(2,1)}), bf16[4,2,65536]{2,1,0:T(2,128)(2,1)S(1)}, u32[]{:S(2)}, u32[]{:S(2)}) %all-to-all-start.3) | async-done | bytes 1048608 | tf_op jit(solution)/shard_map/all_to_all | solution.py:70
  131.5 1.0 fusion.19
  132.6 1.4 copy.44
  134.0 30.8 %all-reduce.2.cloned.1.call-done = f32[8,2048]{1,0:T(8,128)} async-done(((f32[8,2048]{1,0:T(8,128)}), f32[8,2048]{1,0:T(8,128)}) %all-reduce.2.cloned.1.call-update) | async-done | bytes 65552 | tf_op jit(solution)/shard_map/psum | solution.py:77
  164.8 1.0 multiply_reduce_fusion
  165.8 1.6 divide_bitcast_fusion
  (29 shorter events, 5.8 us)
Async XLA Ops:
  9.0 41.4 %copy-start.1 = (s32[1,8]{1,0:T(1,128)S(1)}, s32[1,8]{1,0:T(1,128)}, u32[]{:S(2)}) copy-start(s32[1,8]{1,0:T(1,128)} %param.9) | copy-start | bytes 100
  10.2 18.7 %all-to-all-start.1 = ((bf16[256,4,512]{2,0,1:T(8,128)(2,1)}), bf16[256,4,512]{2,0,1:T(8,128)(2,1)S(1)}, u32[]{:S(2)}, u32[]{:S(2)}) async-start(bf16[256,4,512]{2,0,1:T(8,128)(2,1)} %copy.35), calls=%async_computation.1 | async-start | bytes 2097152 | tf_op jit(solution)/shard_map/all_to_all | solution.py:59
  28.9 18.0 %all-to-all-start.2 = ((bf16[256,4,512]{2,0,1:T(8,128)(2,1)}), bf16[256,4,512]{2,0,1:T(8,128)(2,1)S(1)}, u32[]{:S(2)}, u32[]{:S(2)}) async-start(bf16[256,4,512]{2,0,1:T(8,128)(2,1)} %copy.36), calls=%async_computation.2 | async-start | bytes 2097152 | tf_op jit(solution)/shard_map/all_to_all | solution.py:60
  46.9 18.0 %all-to-all-start = ((bf16[256,4,512]{2,0,1:T(8,128)(2,1)}), bf16[256,4,512]{2,0,1:T(8,128)(2,1)S(1)}, u32[]{:S(2)}, u32[]{:S(2)}) async-start(bf16[256,4,512]{2,0,1:T(8,128)(2,1)} %copy.34), calls=%async_computation | async-start | bytes 2097152 | tf_op jit(solution)/shard_map/all_to_all | solution.py:58
  66.9 7.8 %copy-start = (bf16[1024,4,128]{2,0,1:T(8,128)(2,1)S(1)}, bf16[1024,4,128]{2,0,1:T(8,128)(2,1)}, u32[]{:S(2)}) copy-start(bf16[1024,4,128]{2,0,1:T(8,128)(2,1)} %get-tuple-element.165) | copy-start | bytes 3145732 | tf_op jit(solution)/shard_map/while
  82.5 7.8 %copy-start = (bf16[1024,4,128]{2,0,1:T(8,128)(2,1)S(1)}, bf16[1024,4,128]{2,0,1:T(8,128)(2,1)}, u32[]{:S(2)}) copy-start(bf16[1024,4,128]{2,0,1:T(8,128)(2,1)} %get-tuple-element.165) | copy-start | bytes 3145732 | tf_op jit(solution)/shard_map/while
  111.8 18.0 %all-to-all-start.3 = ((bf16[4,2,65536]{2,1,0:T(2,128)(2,1)}), bf16[4,2,65536]{2,1,0:T(2,128)(2,1)S(1)}, u32[]{:S(2)}, u32[]{:S(2)}) async-start(bf16[4,2,65536]{2,1,0:T(2,128)(2,1)} %reshape.99), calls=%async_computation.3 | async-start | bytes 2097152 | tf_op jit(solution)/shard_map/all_to_all | solution.py:70
  115.3 49.5 %all-reduce.2.cloned.1.call-start = ((), (), s32[]{:S(2)}) async-start(), calls=%async_computation.4 | async-start | bytes 131072 | tf_op jit(solution)/shard_map/psum | solution.py:77
Sparse Core Ops, SparseCore 0:
  132.7 32.0 all-reduce.1
where the time goes:
time: 175 us; the launch traced here: 174 us
  waiting for transfers between devices  77 us (44%)
  local copies, waits for them, and re-layouts  30.4 us (17%)
  matrix products  25.6 us (15%)
  starting transfers between devices  14.8 us (8%)
  between operations  14.2 us (8%)
  other arithmetic  10.7 us (6%)
    psum x1, waiting for transfers between devices, per_device(): sums = lax.psum(token_part, 'seq')  30.8 us
    sub x2, matrix products, one_block(): expo = jnp.exp(scores - top)  15.2 us
    all_to_all x1, waiting for transfers between devices, per_device(): lax.all_to_all(head_rows, 'seq', split_axis=0, concat_axis=1, tiled=True)  14.3 us
    all_to_all x1, waiting for transfers between devices, per_device(): lax.all_to_all(v_split, 'seq', split_axis=1, concat_axis=0, tiled=True)  11.4 us
    all_to_all x1, waiting for transfers between devices, per_device(): lax.all_to_all(k_split, 'seq', split_axis=1, concat_axis=0, tiled=True)  11.4 us
    dot_general x2, matrix products, one_block(): jnp.einsum('hqk,khd->qhd', weights, values_h, preferred_element_type=jnp....  9.36 us
    all_to_all x1, waiting for transfers between devices, per_device(): lax.all_to_all(q_split, 'seq', split_axis=1, concat_axis=0, tiled=True)  9.14 us
    another operation x1, other arithmetic, per_device(): head_rows = head_out.reshape(stream, 1, group_width)  7.04 us
  transfers between devices with their start and end apart: 5, of which 5 were waited for; matrix products, arithmetic and copies ran while one was open for 7% of the time, Pallas kernels for 0%

commit v1 on v0

--- a/solution.py
+++ b/solution.py
@@ -1,6 +1,8 @@
 import jax
 import jax.numpy as jnp
 from jax import lax
+from jax.experimental import pallas as pl
+from jax.experimental.pallas import tpu as pltpu
 from jax.sharding import PartitionSpec as P
 
 HEADS = 16
@@ -42,7 +44,7 @@
     return sums / jnp.sqrt(jnp.mean(sums * sums, axis=-1, keepdims=True) + 1e-06)
 
 
-def per_device(queries, keys, values, lengths):
+def any_axis(queries, keys, values, lengths):
     members = lax.axis_size("seq")
     tok_rows = queries.shape[1]
     width = queries.shape[2]
@@ -78,6 +80,308 @@
     return (rows.reshape(1, tok_rows, width), normalize(sums).reshape(1, doc_count, width))
 
 
+NEG = -1e30
+LOG2E = 1.4426950408889634
+MESH = pl.DeviceIdType.MESH
+
+
+def pair_kernel(
+    lens_ref, q_hbm, k_hbm, v_hbm, out_hbm, dv_ref,
+    q_all, k_all, v_all, bias, send, recv, stat_send, stat_recv,
+    local_out, local_lse, final, sums, peer_sums,
+    own_sem, sib_send, sib_recv, msg_send, msg_recv, st_send, st_recv,
+    out_own, out_send, out_recv, sum_send, sum_recv,
+):
+    me = lax.axis_index("seq")
+    chip = me // 2
+    core = lax.rem(me, 2)
+    sibling = chip * 2 + 1 - core
+    partner = (1 - chip) * 2 + core
+    diagonal = (1 - chip) * 2 + 1 - core
+    tok = q_hbm.shape[1]
+    rows = 2 * tok
+    half = q_hbm.shape[2] // 2
+    heads = half // HD
+    docs = lens_ref.shape[1]
+    factor = LOG2E / HD**0.5
+    blocks = rows // 128
+
+    def column(h):
+        return pl.ds(pl.multiple_of(h * HD, HD), HD)
+
+    def group(g):
+        return pl.ds(pl.multiple_of(g * half, half), half)
+
+    def span(c):
+        return pl.ds(pl.multiple_of(c * tok, tok), tok)
+
+    own_copies = [
+        pltpu.make_async_copy(src.at[0, :, group(core)], dst.at[span(core), :], own_sem.at[i])
+        for i, (src, dst) in enumerate(((q_hbm, q_all), (k_hbm, k_all), (v_hbm, v_all)))
+    ]
+    for copy in own_copies:
+        copy.start()
+
+    barrier = pltpu.get_barrier_semaphore()
+    for other in (sibling, partner, diagonal):
+        pl.semaphore_signal(barrier, inc=1, device_id={"seq": other}, device_id_type=MESH)
+    pl.semaphore_wait(barrier, 3)
+
+    sib_copies = [
+        pltpu.make_async_remote_copy(
+            src_ref=src.at[0, :, group(1 - core)], dst_ref=dst.at[span(core), :],
+            send_sem=sib_send.at[i], recv_sem=sib_recv.at[i],
+            device_id={"seq": sibling}, device_id_type=MESH,
+        )
+        for i, (src, dst) in enumerate(((q_hbm, q_all), (k_hbm, k_all), (v_hbm, v_all)))
+    ]
+    for copy in sib_copies:
+        copy.start()
+
+    ends = []
+    total = jnp.int32(0)
+    for j in range(docs):
+        total = total + lens_ref[0, j]
+        ends.append(total)
+    first = jnp.int32(0)
+    last = jnp.int32(2 * rows)
+    for end in ends:
+        first = jnp.maximum(first, jnp.where(end <= rows, end, 0))
+        last = jnp.minimum(last, jnp.where(end > rows, end, 2 * rows))
+    low = jnp.where(chip == 0, first, 0)
+    high = jnp.where(chip == 0, rows, last - rows)
+
+    def in_cross(index):
+        return (index >= low) & (index < high)
+
+    def message(t, source):
+        return pltpu.make_async_remote_copy(
+            src_ref=source, dst_ref=recv.at[t],
+            send_sem=msg_send.at[t], recv_sem=msg_recv.at[t],
+            device_id={"seq": partner}, device_id_type=MESH,
+        )
+
+    def stats(h):
+        return pltpu.make_async_remote_copy(
+            src_ref=stat_send.at[h], dst_ref=stat_recv.at[h],
+            send_sem=st_send.at[h], recv_sem=st_recv.at[h],
+            device_id={"seq": partner}, device_id_type=MESH,
+        )
+
+    own_copies[0].wait()
+    sib_copies[0].wait_recv()
+    for t in range(2):
+        message(t, q_all.at[:, t * HD : (t + 1) * HD]).start()
+
+    def ids_of(index):
+        ids = jnp.zeros(index.shape, jnp.int32)
+        for end in ends:
+            ids = ids + (end <= index).astype(jnp.int32)
+        return ids
+
+    lane_pos = lax.broadcasted_iota(jnp.int32, (1, rows), 1)
+    lane_ids = ids_of(lane_pos + chip * rows)
+    sub_ids = ids_of(lax.broadcasted_iota(jnp.int32, (rows, 1), 0) + chip * rows)
+    bias[...] = jnp.where(sub_ids == lane_ids, 0.0, NEG)
+    cross_bias = jnp.where(in_cross(lane_pos), 0.0, NEG)
+    onehot = (lane_ids == lax.broadcasted_iota(jnp.int32, (docs, rows), 0)).astype(jnp.bfloat16)
+    eye = lax.broadcasted_iota(jnp.int32, (128, 128), 0) == lax.broadcasted_iota(
+        jnp.int32, (128, 128), 1
+    )
+    ones = jnp.ones((rows, HD), jnp.bfloat16)
+    chunk = min(CHUNK, rows)
+
+    for i in (1, 2):
+        own_copies[i].wait()
+        sib_copies[i].wait_recv()
+
+    def mix(q, h, bias_rows):
+        scores = lax.dot_general(
+            q, k_all[:, column(h)], (((1,), (1,)), ((), ())), preferred_element_type=jnp.float32
+        )
+        scores = scores * factor + bias_rows
+        top = jnp.max(scores, axis=1, keepdims=True)
+        expo = jnp.exp2(scores - top).astype(jnp.bfloat16)
+        wide = jnp.concatenate([v_all[:, column(h)], ones], axis=1)
+        both = jnp.dot(expo, wide, preferred_element_type=jnp.float32)
+        mass = both[:, HD:]
+        return both[:, :HD] / mass, top + jnp.log2(mass)
+
+    def local(h):
+        for start in range(0, rows, chunk):
+            part = slice(start, start + chunk)
+            out, lse = mix(q_all[part, column(h)], h, bias[part, :])
+            local_out[h, part, :] = out
+            local_lse[h, part, :] = lse
+
+    def remote(h, with_query):
+        t = h + 2
+        message(h, send.at[h]).wait_recv()
+        for start in range(0, rows, chunk):
+            part = slice(start, start + chunk)
+            out, lse = mix(recv[h, part, :], h, cross_bias)
+            out = out.astype(jnp.bfloat16)
+            if with_query:
+                index = start + lax.broadcasted_iota(jnp.int32, (chunk, HD), 0)
+                out = jnp.where(in_cross(index), q_all[part, column(t)].astype(jnp.float32), out.astype(jnp.float32)).astype(jnp.bfloat16)
+            send[t, part, :] = out
+            for i in range(chunk // 128):
+                block = jnp.where(eye, lse[i * 128 : (i + 1) * 128, :], 0.0)
+                at = start // 128 + i
+                stat_send[h, at : at + 1, :] = jnp.sum(block, axis=0, keepdims=True)
+        message(t, send.at[t]).start()
+        stats(h).start()
+
+    def out_copy(h):
+        where = pl.ds(pl.multiple_of(core * half + h * HD, HD), HD)
+        keep = pltpu.make_async_copy(
+            final.at[h, span(core), :], out_hbm.at[0, :, where], out_own.at[h]
+        )
+        give = pltpu.make_async_remote_copy(
+            src_ref=final.at[h, span(1 - core), :], dst_ref=out_hbm.at[0, :, where],
+            send_sem=out_send.at[h], recv_sem=out_recv.at[h],
+            device_id={"seq": sibling}, device_id_type=MESH,
+        )
+        return keep, give
+
+    def combine(h):
+        stats(h).wait_recv()
+        for i in range(blocks):
+            part = slice(i * 128, (i + 1) * 128)
+            line = jnp.broadcast_to(stat_recv[h, i : i + 1, :], (128, 128))
+            other = jnp.sum(jnp.where(eye, line, 0.0), axis=1, keepdims=True)
+            index = i * 128 + lax.broadcasted_iota(jnp.int32, (128, HD), 0)
+            gap = jnp.where(in_cross(index), local_lse[h, part, :] - other, 200.0)
+            share = 1.0 / (1.0 + jnp.exp2(jnp.minimum(gap, 100.0)))
+            share = jnp.where(gap > 99.0, 0.0, share)
+            mine = local_out[h, part, :]
+            theirs = recv[h + 2, part, :].astype(jnp.float32)
+            final[h, part, :] = (mine + share * (theirs - mine)).astype(jnp.bfloat16)
+        for copy in out_copy(h):
+            copy.start()
+        sums[:, column(h)] = jnp.dot(onehot, final[h], preferred_element_type=jnp.float32)
+
+    def loop(begin, end, body):
+        def step(h, carry):
+            body(h)
+            return carry
+
+        lax.fori_loop(begin, end, step, 0)
+
+    def opening(h):
+        remote(h, True)
+        local(h + 2)
+
+    def middle(h):
+        remote(h, True)
+        local(h + 2)
+        combine(h - 2)
+
+    def closing(h):
+        remote(h, False)
+        combine(h - 2)
+
+    loop(0, 2, local)
+    loop(0, 2, opening)
+    loop(2, heads - 2, middle)
+    loop(heads - 2, heads, closing)
+    for h in (heads - 2, heads - 1):
+        message(h + 2, send.at[h + 2]).wait_recv()
+        combine(h)
+
+    sum_copies = [
+        pltpu.make_async_remote_copy(
+            src_ref=sums, dst_ref=peer_sums.at[i],
+            send_sem=sum_send.at[i], recv_sem=sum_recv.at[i],
+            device_id={"seq": other}, device_id_type=MESH,
+        )
+        for i, other in enumerate((partner, sibling, diagonal))
+    ]
+    for copy in sum_copies:
+        copy.start()
+
+    for copy in sib_copies:
+        copy.wait_send()
+
+    def finish(t):
+        message(t, send.at[t]).wait_send()
+
+    loop(0, heads + 2, finish)
+
+    def finish_head(h):
+        stats(h).wait_send()
+        keep, give = out_copy(h)
+        keep.wait()
+        give.wait_send()
+        give.wait_recv()
+
+    loop(0, heads, finish_head)
+    for copy in sum_copies:
+        copy.wait()
+    here = sums[...] + peer_sums[0]
+    there = peer_sums[1] + peer_sums[2]
+    square = jnp.sum(here * here, axis=1, keepdims=True) + jnp.sum(
+        there * there, axis=1, keepdims=True
+    )
+    root = jnp.sqrt(square / (2 * half) + 1e-06)
+    dv_ref[0, :, group(core)] = here / root
+    dv_ref[0, :, group(1 - core)] = there / root
+
+
+CHUNK = 256
+
+
+def two_chips(queries, keys, values, lengths):
+    _, tok, width = queries.shape
+    rows, half, docs = 2 * tok, width // 2, lengths.shape[1]
+    heads = half // HD
+    bf, f32 = jnp.bfloat16, jnp.float32
+    dma = pltpu.SemaphoreType.DMA
+    hbm = pl.BlockSpec(memory_space=pl.ANY)
+    return pl.pallas_call(
+        pair_kernel,
+        out_shape=(
+            jax.ShapeDtypeStruct(queries.shape, bf),
+            jax.ShapeDtypeStruct((1, docs, width), f32),
+        ),
+        in_specs=[pl.BlockSpec(memory_space=pltpu.SMEM), hbm, hbm, hbm],
+        out_specs=(hbm, pl.BlockSpec(memory_space=pltpu.VMEM)),
+        scratch_shapes=[
+            pltpu.VMEM((rows, half), bf),
+            pltpu.VMEM((rows, half), bf),
+            pltpu.VMEM((rows, half), bf),
+            pltpu.VMEM((rows, rows), f32),
+            pltpu.VMEM((heads + 2, rows, HD), bf),
+            pltpu.VMEM((heads + 2, rows, HD), bf),
+            pltpu.VMEM((heads, max(rows // 128, 8), 128), f32),
+            pltpu.VMEM((heads, max(rows // 128, 8), 128), f32),
+            pltpu.VMEM((heads, rows, HD), f32),
+            pltpu.VMEM((heads, rows, HD), f32),
+            pltpu.VMEM((heads, rows, HD), bf),
+            pltpu.VMEM((docs, half), f32),
+            pltpu.VMEM((3, docs, half), f32),
+            dma((3,)), dma((3,)), dma((3,)),
+            dma((heads + 2,)), dma((heads + 2,)),
+            dma((heads,)), dma((heads,)),
+            dma((heads,)), dma((heads,)), dma((heads,)),
+            dma((3,)), dma((3,)),
+        ],
+        compiler_params=pltpu.CompilerParams(
+            collective_id=0, has_side_effects=True, vmem_limit_bytes=48 * 1024 * 1024
+        ),
+        cost_estimate=pl.CostEstimate(
+            flops=8 * heads * rows * rows * HD, bytes_accessed=8 * tok * width,
+            transcendentals=2 * heads * rows * rows,
+        ),
+    )(lengths, queries, keys, values)
+
+
+def per_device(queries, keys, values, lengths):
+    if lax.axis_size("seq") == 4:
+        return two_chips(queries, keys, values, lengths)
+    return any_axis(queries, keys, values, lengths)
+
+
 def solution(mesh):
     return jax.shard_map(
         per_device,

time: 175 us -> 47.1 us (0.27)
  waiting for transfers between devices: 77 us -> 0 us
  Pallas kernels: 0 us -> 40.3 us
  matrix products: 25.6 us -> 0 us
  local copies, waits for them, and re-layouts: 30.4 us -> 5.92 us
  starting transfers between devices: 14.8 us -> 0 us
  between operations: 14.2 us -> 0.65 us
  other arithmetic: 10.7 us -> 0 us
    all_to_all x4 -> x0, waiting for transfers between devices: 46.2 us -> none  [the longest x1 14.3 us: per_device(): lax.all_to_all(head_rows, 'seq', split_axis=0, concat_axis=1, tiled=True)]
    pallas_call x0 -> x1, Pallas kernels: none -> 40.3 us  [two_chips(): pl.pallas_call(pair_kernel, out_shape=(jax.ShapeDtypeStruct(queries.shape...]
    psum x1 -> x0, waiting for transfers between devices: 30.8 us -> none  [per_device(): sums = lax.psum(token_part, 'seq')]
    another operation x8 -> x0, local copies, waits for them, and re-layouts: 15.7 us -> none  [the longest x2 6.54 us: per_device(): head_rows = head_out.reshape(stream, 1, group_width)]
    sub x2 -> x0, matrix products: 15.2 us -> none  [one_block(): expo = jnp.exp(scores - top)]
    all_to_all x4 -> x0, starting transfers between devices: 14.8 us -> none  [the longest x1 4.24 us: per_device(): lax.all_to_all(k_split, 'seq', split_axis=1, concat_axis=0, tiled=True)]
    dot_general x3 -> x0, matrix products: 10.4 us -> none  [the longest x2 9.36 us: one_block(): jnp.einsum('hqk,khd->qhd', weights, values_h, preferred_element_type=jnp....]
    another operation x2 -> x0, other arithmetic: 7.23 us -> none  [the longest x1 7.04 us: per_device(): head_rows = head_out.reshape(stream, 1, group_width)]
  transfers between devices with their start and end apart: 5 -> 0, of which waited for: 5 -> 0; matrix products, arithmetic and copies ran while one was open for 7% -> 0% of each run, Pallas kernels for 0% -> 0%
where the time goes in v1:
time: 47.1 us; the launch traced here: 46.8 us
  Pallas kernels  40.3 us (86%)
  local copies, waits for them, and re-layouts  5.92 us (13%)
  between operations  0.65 us (1%)
    pallas_call x1, Pallas kernels, two_chips(): pl.pallas_call(pair_kernel, out_shape=(jax.ShapeDtypeStruct(queries.shape...  40.3 us
    unnamed x10, local copies, waits for them, and re-layouts  5.92 us

profile of v1, /device:TPU:0, one launch (start us, length us, event | category | flops | bytes accessed | tf_op | source)
XLA Modules:
  0.0 46.8 jit_solution(10486404539550342871)
XLA Ops:
  0.6 0.0 copy-start
  0.6 1.2 %copy-done = bf16[1,256,2048]{2,1,0:T(8,128)(2,1)S(1)} copy-done((bf16[1,256,2048]{2,1,0:T(8,128)(2,1)S(1)}, bf16[1,256,2048]{2,1,0:T(8,128)(2,1)}, u32[]{:S(2)}) %copy-start) | copy-done | bytes 1048600
  1.9 0.0 copy-start.1
  1.9 1.2 %copy-done.1 = bf16[1,256,2048]{2,1,0:T(8,128)(2,1)S(1)} copy-done((bf16[1,256,2048]{2,1,0:T(8,128)(2,1)S(1)}, bf16[1,256,2048]{2,1,0:T(8,128)(2,1)}, u32[]{:S(2)}) %copy-start.1) | copy-done | bytes 1048600
  3.1 0.0 copy-start.2
  3.1 1.2 %copy-done.2 = bf16[1,256,2048]{2,1,0:T(8,128)(2,1)S(1)} copy-done((bf16[1,256,2048]{2,1,0:T(8,128)(2,1)S(1)}, bf16[1,256,2048]{2,1,0:T(8,128)(2,1)}, u32[]{:S(2)}) %copy-start.2) | copy-done | bytes 1048600
  4.3 0.0 copy-start.3
  4.3 0.7 %copy-done.3 = s32[1,8]{1,0:T(1,128)S(1)} copy-done((s32[1,8]{1,0:T(1,128)S(1)}, s32[1,8]{1,0:T(1,128)}, u32[]{:S(2)}) %copy-start.3) | copy-done | bytes 56
  5.0 40.3 %shard_map.59 = (bf16[1,256,2048]{2,1,0:T(8,128)(2,1)S(1)}, f32[1,8,2048]{2,1,0:T(8,128)S(1)}) custom-call(s32[1,8]{1,0:T(1,128)S(1)} %copy-done.3, bf16[1,256,2048]{2,1,0:T(8,128)(2,1)S(1)} %copy-done, bf16[1,256,2048]{2,1,0:T(8,128)(2,1)S(1)} %copy-done.1, bf16[1,256,2048]{2,1,0:T(8,128)(2,1)S(1)} %copy-done.2), custom_call_target="tpu_custom_call" | custom-call | flops 2147483648 | bytes 4194304 | tf_op jit(solution)/shard_map/pallas_call | solution.py:341
  45.2 1.0 %copy.8 = bf16[1,256,2048]{2,1,0:T(8,128)(2,1)} copy(bf16[1,256,2048]{2,1,0:T(8,128)(2,1)S(1)} %get-tuple-element.4) | data formatting | bytes 2097152
  46.2 0.6 %copy.9 = f32[1,8,2048]{2,1,0:T(8,128)} copy(f32[1,8,2048]{2,1,0:T(8,128)S(1)} %get-tuple-element.5) | data formatting | bytes 131072
Async XLA Ops:
  0.6 1.2 %copy-start = (bf16[1,256,2048]{2,1,0:T(8,128)(2,1)S(1)}, bf16[1,256,2048]{2,1,0:T(8,128)(2,1)}, u32[]{:S(2)}) copy-start(bf16[1,256,2048]{2,1,0:T(8,128)(2,1)} %q_hbm.1) | copy-start | bytes 3145732
  1.9 1.2 %copy-start.1 = (bf16[1,256,2048]{2,1,0:T(8,128)(2,1)S(1)}, bf16[1,256,2048]{2,1,0:T(8,128)(2,1)}, u32[]{:S(2)}) copy-start(bf16[1,256,2048]{2,1,0:T(8,128)(2,1)} %k_hbm.1) | copy-start | bytes 3145732
  3.1 1.2 %copy-start.2 = (bf16[1,256,2048]{2,1,0:T(8,128)(2,1)S(1)}, bf16[1,256,2048]{2,1,0:T(8,128)(2,1)}, u32[]{:S(2)}) copy-start(bf16[1,256,2048]{2,1,0:T(8,128)(2,1)} %v_hbm.1) | copy-start | bytes 3145732
  4.3 0.7 %copy-start.3 = (s32[1,8]{1,0:T(1,128)S(1)}, s32[1,8]{1,0:T(1,128)}, u32[]{:S(2)}) copy-start(s32[1,8]{1,0:T(1,128)} %lens_ref.1) | copy-start | bytes 100

commit v2 on v1

v2 whole, which is shorter than its diff:
```python
import jax
import jax.numpy as jnp
from jax import lax
from jax.experimental import pallas as pl
from jax.experimental.pallas import tpu as pltpu
from jax.sharding import PartitionSpec as P

HEADS = 16
HD = 128


def doc_index(lens, positions):
    ends = jnp.cumsum(lens)
    return jnp.sum((ends[None, :] <= positions[:, None]).astype(jnp.int32), axis=1)


def attend(queries_h, keys_h, values_h, doc_ids):
    stream = queries_h.shape[0]
    block = 512
    count = stream // block
    scale = 1.0 / queries_h.shape[2] ** 0.5

    def one_block(index):
        start = index * block
        q_block = lax.dynamic_slice_in_dim(queries_h, start, block, 0)
        ids = lax.dynamic_slice_in_dim(doc_ids, start, block, 0)
        scores = (
            jnp.einsum("qhd,khd->hqk", q_block, keys_h, preferred_element_type=jnp.float32) * scale
        )
        same = ids[:, None] == doc_ids[None, :]
        scores = jnp.where(same[None], scores, -1e30)
        top = jnp.max(scores, axis=2, keepdims=True)
        expo = jnp.exp(scores - top)
        probs = expo / jnp.sum(expo, axis=2, keepdims=True)
        weights = probs.astype(jnp.bfloat16)
        mixed = jnp.einsum("hqk,khd->qhd", weights, values_h, preferred_element_type=jnp.float32)
        return mixed.astype(jnp.bfloat16)

    out = lax.map(one_block, jnp.arange(count, dtype=jnp.int32))
    return out.reshape(stream, queries_h.shape[1], queries_h.shape[2])


def normalize(sums):
    return sums / jnp.sqrt(jnp.mean(sums * sums, axis=-1, keepdims=True) + 1e-06)


def any_axis(queries, keys, values, lengths):
    members = lax.axis_size("seq")
    tok_rows = queries.shape[1]
    width = queries.shape[2]
    local_heads = HEADS // members
    group_width = local_heads * HD
    stream = tok_rows * members
    lens = lengths[0]
    doc_count = lens.shape[0]
    q_split = queries[0].reshape(tok_rows, members, group_width)
    k_split = keys[0].reshape(tok_rows, members, group_width)
    v_split = values[0].reshape(tok_rows, members, group_width)
    q_heads, k_heads, v_heads = (
        lax.all_to_all(q_split, "seq", split_axis=1, concat_axis=0, tiled=True),
        lax.all_to_all(k_split, "seq", split_axis=1, concat_axis=0, tiled=True),
        lax.all_to_all(v_split, "seq", split_axis=1, concat_axis=0, tiled=True),
    )
    all_ids = doc_index(lens, jnp.arange(stream, dtype=jnp.int32))
    head_out = attend(
        q_heads.reshape(stream, local_heads, HD),
        k_heads.reshape(stream, local_heads, HD),
        v_heads.reshape(stream, local_heads, HD),
        all_ids,
    )
    head_rows = head_out.reshape(stream, 1, group_width)
    back = lax.all_to_all(head_rows, "seq", split_axis=0, concat_axis=1, tiled=True)
    rows = back.reshape(tok_rows, width)
    doc_range = jnp.arange(doc_count, dtype=jnp.int32)
    start = lax.axis_index("seq") * tok_rows
    local_ids = doc_index(lens, start + jnp.arange(tok_rows, dtype=jnp.int32))
    onehot_local = (local_ids[None, :] == doc_range[:, None]).astype(jnp.bfloat16)
    token_part = jnp.dot(onehot_local, rows, preferred_element_type=jnp.float32)
    sums = lax.psum(token_part, "seq")
    return (rows.reshape(1, tok_rows, width), normalize(sums).reshape(1, doc_count, width))


NEG = -1e30
LOG2E = 1.4426950408889634
MESH = pl.DeviceIdType.MESH


def pair_kernel(
    lens_hbm, q_hbm, k_hbm, v_hbm, out_hbm, dv_ref,
    lens, q_all, k_all, v_all, bias, send, recv, stat_send, stat_recv,
    local_out, local_lse, final, expo_last, top_last, sums, peer_sums,
    lens_sem, own_sem, sib_send, sib_recv, early_send, early_recv, msg_send, msg_recv,
    st_send, st_recv, out_own, out_send, out_recv, sum_send, sum_recv,
):
    me = lax.axis_index("seq")
    chip = me // 2
    core = lax.rem(me, 2)
    sibling = chip * 2 + 1 - core
    partner = (1 - chip) * 2 + core
    diagonal = (1 - chip) * 2 + 1 - core
    tok = q_hbm.shape[1]
    rows = 2 * tok
    half = q_hbm.shape[2] // 2
    heads = half // HD
    docs = lens.shape[1]
    factor = LOG2E / HD**0.5
    pieces = rows // PIECE
    blocks = PIECE // 128

    def column(h):
        return pl.ds(pl.multiple_of(h * HD, HD), HD)

    def group(g):
        return pl.ds(pl.multiple_of(g * half, half), half)

    def span(c):
        return pl.ds(pl.multiple_of(c * tok, tok), tok)

    lens_copy = pltpu.make_async_copy(lens_hbm, lens, lens_sem)
    lens_copy.start()
    own_copies = [
        pltpu.make_async_copy(src.at[0, :, group(core)], dst.at[span(core), :], own_sem.at[i])
        for i, (src, dst) in enumerate(((k_hbm, k_all), (v_hbm, v_all), (q_hbm, q_all)))
    ]
    for copy in own_copies:
        copy.start()

    barrier = pltpu.get_barrier_semaphore()
    for other in (sibling, partner, diagonal):
        pl.semaphore_signal(barrier, inc=1, device_id={"seq": other}, device_id_type=MESH)
    pl.semaphore_wait(barrier, 3)

    def early(t, i, there, g):
        return pltpu.make_async_remote_copy(
            src_ref=q_hbm.at[0, :, pl.ds(pl.multiple_of(g * half + t * HD, HD), HD)],
            dst_ref=recv.at[t, span(core), :],
            send_sem=early_send.at[t, i], recv_sem=early_recv.at[t, core],
            device_id={"seq": there}, device_id_type=MESH,
        )

    early_copies = [
        early(t, i, *to) for t in range(2) for i, to in enumerate(((partner, core), (diagonal, 1 - core)))
    ]
    for copy in early_copies:
        copy.start()
    sib_copies = [
        pltpu.make_async_remote_copy(
            src_ref=src.at[0, :, group(1 - core)], dst_ref=dst.at[span(core), :],
            send_sem=sib_send.at[i], recv_sem=sib_recv.at[i],
            device_id={"seq": sibling}, device_id_type=MESH,
        )
        for i, (src, dst) in enumerate(((k_hbm, k_all), (v_hbm, v_all), (q_hbm, q_all)))
    ]
    for copy in sib_copies:
        copy.start()

    lens_copy.wait()
    ends = []
    total = jnp.int32(0)
    for j in range(docs):
        total = total + lens[0, j]
        ends.append(total)
    first = jnp.int32(0)
    last = jnp.int32(2 * rows)
    for end in ends:
        first = jnp.maximum(first, jnp.where(end <= rows, end, 0))
        last = jnp.minimum(last, jnp.where(end > rows, end, 2 * rows))
    low = jnp.where(chip == 0, first, 0)
    high = jnp.where(chip == 0, rows, last - rows)

    other_low = jnp.where(chip == 0, 0, first)
    other_high = jnp.where(chip == 0, last - rows, rows)

    def in_cross(index):
        return (index >= low) & (index < high)

    def ids_of(index):
        ids = jnp.zeros(index.shape, jnp.int32)
        for end in ends:
            ids = ids + (end <= index).astype(jnp.int32)
        return ids

    lane_pos = lax.broadcasted_iota(jnp.int32, (1, rows), 1)
    lane_ids = ids_of(lane_pos + chip * rows)
    sub_ids = ids_of(lax.broadcasted_iota(jnp.int32, (rows, 1), 0) + chip * rows)
    bias[...] = jnp.where(sub_ids == lane_ids, 0.0, NEG)
    cross_bias = jnp.where(in_cross(lane_pos), 0.0, NEG)
    other_bias = jnp.where((lane_pos >= other_low) & (lane_pos < other_high), 0.0, NEG)
    onehot = (lane_ids == lax.broadcasted_iota(jnp.int32, (docs, rows), 0)).astype(jnp.bfloat16)
    eye = lax.broadcasted_iota(jnp.int32, (128, 128), 0) == lax.broadcasted_iota(
        jnp.int32, (128, 128), 1
    )
    ones = jnp.ones((rows, HD), jnp.bfloat16)

    def part_of(p):
        return slice(p * PIECE, (p + 1) * PIECE)

    def message(t, p):
        return pltpu.make_async_remote_copy(
            src_ref=send.at[t, part_of(p), :], dst_ref=recv.at[t, part_of(p), :],
            send_sem=msg_send.at[t, p], recv_sem=msg_recv.at[t, p],
            device_id={"seq": partner}, device_id_type=MESH,
        )

    def stats(h):
        return pltpu.make_async_remote_copy(
            src_ref=stat_send.at[h], dst_ref=stat_recv.at[h],
            send_sem=st_send.at[h], recv_sem=st_recv.at[h],
            device_id={"seq": partner}, device_id_type=MESH,
        )

    def expo_of(q, keys, bias_rows):
        scores = lax.dot_general(
            q, keys, (((1,), (1,)), ((), ())), preferred_element_type=jnp.float32
        )
        scores = scores * factor + bias_rows
        top = jnp.max(scores, axis=1, keepdims=True)
        return jnp.exp2(scores - top).astype(jnp.bfloat16), top

    def weigh(expo, top, vals):
        wide = jnp.concatenate([vals, ones], axis=1)
        both = jnp.dot(expo, wide, preferred_element_type=jnp.float32)
        mass = both[:, HD:]
        return both[:, :HD] / mass, top + jnp.log2(mass)

    def mix(q, h, bias_rows):
        expo, top = expo_of(q, k_all[:, column(h)], bias_rows)
        return weigh(expo, top, v_all[:, column(h)])

    def local(h, p):
        part = part_of(p)
        out, lse = mix(q_all[part, column(h)], h, bias[part, :])
        local_out[h, part, :] = out
        local_lse[h, part, :] = lse

    def remote(h, p, source, at):
        part = part_of(p)
        out, lse = mix(recv[h, part, :], h, cross_bias)
        index = p * PIECE + lax.broadcasted_iota(jnp.int32, (PIECE, HD), 0)
        own = source[part, column(at)].astype(jnp.float32)
        send[h + 2, part, :] = jnp.where(in_cross(index), own, out).astype(jnp.bfloat16)
        message(h + 2, p).start()
        for i in range(blocks):
            block = jnp.where(eye, lse[i * 128 : (i + 1) * 128, :], 0.0)
            row = p * blocks + i
            stat_send[h, row : row + 1, :] = jnp.sum(block, axis=0, keepdims=True)

    def out_copy(h):
        where = pl.ds(pl.multiple_of(core * half + h * HD, HD), HD)
        keep = pltpu.make_async_copy(
            final.at[h, span(core), :], out_hbm.at[0, :, where], out_own.at[h]
        )
        give = pltpu.make_async_remote_copy(
            src_ref=final.at[h, span(1 - core), :], dst_ref=out_hbm.at[0, :, where],
            send_sem=out_send.at[h], recv_sem=out_recv.at[h],
            device_id={"seq": sibling}, device_id_type=MESH,
        )
        return keep, give

    def blend(h, start, size, theirs, other):
        part = slice(start, start + size)
        index = start + lax.broadcasted_iota(jnp.int32, (size, HD), 0)
        gap = jnp.where(in_cross(index), local_lse[h, part, :] - other, 200.0)
        share = 1.0 / (1.0 + jnp.exp2(jnp.minimum(gap, 100.0)))
        share = jnp.where(gap > 99.0, 0.0, share)
        mine = local_out[h, part, :]
        final[h, part, :] = (mine + share * (theirs - mine)).astype(jnp.bfloat16)

    def combine(h, p):
        for i in range(p * blocks, (p + 1) * blocks):
            line = jnp.broadcast_to(stat_recv[h, i : i + 1, :], (128, 128))
            other = jnp.sum(jnp.where(eye, line, 0.0), axis=1, keepdims=True)
            theirs = recv[h + 2, i * 128 : (i + 1) * 128, :].astype(jnp.float32)
            blend(h, i * 128, 128, theirs, other)

    def close(h):
        for copy in out_copy(h):
            copy.start()
        sums[:, column(h)] = jnp.dot(onehot, final[h], preferred_element_type=jnp.float32)

    def early_in(t, c):
        part = recv.at[t, c * tok : (c + 1) * tok, :]
        pltpu.make_async_remote_copy(
            src_ref=part, dst_ref=part,
            send_sem=early_send.at[t, 0], recv_sem=early_recv.at[t, c],
            device_id={"seq": partner}, device_id_type=MESH,
        ).wait_recv()

    def step(h, source, at, opening=False):
        for p in range(pieces):
            if not opening:
                message(h, p).wait_recv()
            elif p * PIECE % tok == 0:
                early_in(h, p * PIECE // tok)
            remote(h, p, source, at)
        stats(h).start()
        for p in range(pieces):
            local(h, p)
        if not opening:
            settle(h - 2)

    def settle(h):
        stats(h).wait_recv()
        for p in range(pieces):
            combine(h, p)
        close(h)

    for i in range(3):
        own_copies[i].wait()
        sib_copies[i].wait_recv()
    end = heads - 1
    step(0, q_all, 2, opening=True)
    step(1, q_all, 3, opening=True)

    def middle(h, carry):
        step(h, q_all, h + 2)
        return carry

    lax.fori_loop(2, heads - 3, middle, 0)
    step(heads - 3, k_all, end)
    step(heads - 2, v_all, end)
    for p in range(pieces):
        local(end, p)

    def sum_copy(n, i, other, begin, end):
        return pltpu.make_async_remote_copy(
            src_ref=sums.at[:, begin * HD : end * HD],
            dst_ref=peer_sums.at[i, :, begin * HD : end * HD],
            send_sem=sum_send.at[n, i], recv_sem=sum_recv.at[n, i],
            device_id={"seq": other}, device_id_type=MESH,
        )

    sum_copies = [
        [sum_copy(n, i, other, *cut) for i, other in enumerate((partner, diagonal, sibling))]
        for n, cut in enumerate(((0, heads - 2), (heads - 2, heads)))
    ]
    for p in range(pieces):
        message(end, p).wait_recv()
    for p in range(pieces):
        expo, top = expo_of(q_all[part_of(p), column(end)], recv[end], other_bias)
        expo_last[part_of(p), :] = expo
        top_last[part_of(p), :] = jnp.broadcast_to(top, (PIECE, HD))
    settle(end - 2)
    for copy in sum_copies[0]:
        copy.start()

    for p in range(pieces):
        message(heads, p).wait_recv()
    for p in range(pieces):
        part = part_of(p)
        theirs, other = weigh(expo_last[part, :], top_last[part, :], recv[heads])
        blend(end, p * PIECE, PIECE, theirs, other)
    close(end)
    settle(end - 1)
    for copy in sum_copies[1]:
        copy.start()

    for copy in sib_copies + early_copies:
        copy.wait_send()

    def finish_message(h, carry):
        for p in range(pieces):
            message(h + 2, p).wait_send()
        stats(h).wait_send()
        return carry

    def finish_head(h, carry):
        keep, give = out_copy(h)
        keep.wait()
        give.wait_send()
        give.wait_recv()
        return carry

    lax.fori_loop(0, end, finish_message, 0)
    lax.fori_loop(0, heads, finish_head, 0)
    for copy in sum_copies[0] + sum_copies[1]:
        copy.wait()
    here = sums[...] + peer_sums[0]
    there = peer_sums[1] + peer_sums[2]
    square = jnp.sum(here * here, axis=1, keepdims=True) + jnp.sum(
        there * there, axis=1, keepdims=True
    )
    root = jnp.sqrt(square / (2 * half) + 1e-06)
    dv_ref[0, :, group(core)] = here / root
    dv_ref[0, :, group(1 - core)] = there / root


PIECE = 256
LIMIT = 65536 - 1280


def two_chips(queries, keys, values, lengths):
    _, tok, width = queries.shape
    rows, half, docs = 2 * tok, width // 2, lengths.shape[1]
    heads = half // HD
    bf, f32 = jnp.bfloat16, jnp.float32
    dma = pltpu.SemaphoreType.DMA
    hbm = pl.BlockSpec(memory_space=pl.ANY)
    return pl.pallas_call(
        pair_kernel,
        out_shape=(
            jax.ShapeDtypeStruct(queries.shape, bf),
            jax.ShapeDtypeStruct((1, docs, width), f32),
        ),
        in_specs=[hbm, hbm, hbm, hbm],
        out_specs=(hbm, pl.BlockSpec(memory_space=pltpu.VMEM)),
        scratch_shapes=[
            pltpu.SMEM(lengths.shape, jnp.int32),
            pltpu.VMEM((rows, half), bf),
            pltpu.VMEM((rows, half), bf),
            pltpu.VMEM((rows, half), bf),
            pltpu.VMEM((rows, rows), f32),
            pltpu.VMEM((heads + 1, rows, HD), bf),
            pltpu.VMEM((heads + 1, rows, HD), bf),
            pltpu.VMEM((heads, max(rows // 128, 8), 128), f32),
            pltpu.VMEM((heads, max(rows // 128, 8), 128), f32),
            pltpu.VMEM((heads, rows, HD), f32),
            pltpu.VMEM((heads, rows, HD), f32),
            pltpu.VMEM((heads, rows, HD), bf),
            pltpu.VMEM((rows, rows), bf),
            pltpu.VMEM((rows, HD), f32),
            pltpu.VMEM((docs, half), f32),
            pltpu.VMEM((3, docs, half), f32),
            dma, dma((3,)), dma((3,)), dma((3,)), dma((2, 2)), dma((2, 2)),
            dma((heads + 1, rows // PIECE)), dma((heads + 1, rows // PIECE)),
            dma((heads,)), dma((heads,)),
            dma((heads,)), dma((heads,)), dma((heads,)),
            dma((2, 3)), dma((2, 3)),
        ],
        compiler_params=pltpu.CompilerParams(
            collective_id=0, has_side_effects=True, vmem_limit_bytes=LIMIT * 1024
        ),
        cost_estimate=pl.CostEstimate(
            flops=8 * heads * rows * rows * HD, bytes_accessed=8 * tok * width,
            transcendentals=2 * heads * rows * rows,
        ),
    )(lengths, queries, keys, values)


def per_device(queries, keys, values, lengths):
    if lax.axis_size("seq") == 4:
        return two_chips(queries, keys, values, lengths)
    return any_axis(queries, keys, values, lengths)


def solution(mesh):
    return jax.shard_map(
        per_device,
        mesh=mesh,
        in_specs=(
            P(("rep", "dp"), "seq", None),
            P(("rep", "dp"), "seq", None),
            P(("rep", "dp"), "seq", None),
            P(("rep", "dp"), None),
        ),
        out_specs=(P(("rep", "dp"), "seq", None), P(("rep", "dp"), None, None)),
        check_vma=False,
    )
```

time: 47.1 us -> 40.5 us (0.86)
  Pallas kernels: 40.3 us -> 36.8 us
  local copies, waits for them, and re-layouts: 5.92 us -> 2.97 us
    pallas_call x1, Pallas kernels: 40.3 us -> 36.8 us  [two_chips(): pl.pallas_call(pair_kernel, out_shape=(jax.ShapeDtypeStruct(queries.shape...]
    unnamed x10 -> x4, local copies, waits for them, and re-layouts: 5.92 us -> 2.97 us
where the time goes in v2:
time: 40.5 us; the launch traced here: 40.4 us
  Pallas kernels  36.8 us (91%)
  local copies, waits for them, and re-layouts  2.97 us (7%)
  between operations  0.65 us (2%)
    pallas_call x1, Pallas kernels, two_chips(): pl.pallas_call(pair_kernel, out_shape=(jax.ShapeDtypeStruct(queries.shape...  36.8 us
    unnamed x4, local copies, waits for them, and re-layouts  2.97 us

profile of v2, /device:TPU:0, one launch (start us, length us, event | category | flops | bytes accessed | tf_op | source)
XLA Modules:
  0.0 40.4 jit_solution(3843581474773705101)
XLA Ops:
  0.6 36.8 %shard_map.59 = (bf16[1,256,2048]{2,1,0:T(8,128)(2,1)}, f32[1,8,2048]{2,1,0:T(8,128)}) custom-call(s32[1,8]{1,0:T(1,128)} %lens_hbm.1, bf16[1,256,2048]{2,1,0:T(8,128)(2,1)} %q_hbm.1, bf16[1,256,2048]{2,1,0:T(8,128)(2,1)} %k_hbm.1, bf16[1,256,2048]{2,1,0:T(8,128)(2,1)} %v_hbm.1), custom_call_target="tpu_custom_call" | custom-call | flops 2147483648 | bytes 4194304 | tf_op jit(solution)/shard_map/pallas_call | solution.py:399
  37.4 0.0 copy-start
  37.4 2.3 %copy.8 = bf16[1,256,2048]{2,1,0:T(8,128)(2,1)} copy(bf16[1,256,2048]{2,1,0:T(8,128)(2,1)} %get-tuple-element.4) | data formatting | bytes 2097152
  39.7 0.0 copy-done
  39.7 0.6 %copy.9 = f32[1,8,2048]{2,1,0:T(8,128)} copy(f32[1,8,2048]{2,1,0:T(8,128)S(1)} %copy-done) | data formatting | bytes 131072
Async XLA Ops:
  37.4 2.3 %copy-start = (f32[1,8,2048]{2,1,0:T(8,128)S(1)}, f32[1,8,2048]{2,1,0:T(8,128)}, u32[]{:S(2)}) copy-start(f32[1,8,2048]{2,1,0:T(8,128)} %get-tuple-element.5) | copy-start | bytes 196612

commit v3 on v2

--- a/solution.py
+++ b/solution.py
@@ -386,7 +386,27 @@
 
 
 PIECE = 256
-LIMIT = 65536 - 1280
+SHARES = 4
+LIMIT = 65536 - 128
+
+
+def hand_over(rows_in, vec_in, rows_out, vec_out, rows_held, vec_held, sems_in, sems_out):
+    share = rows_in.shape[1] // SHARES
+    legs = []
+    for i in range(SHARES):
+        part = slice(i * share, (i + 1) * share)
+        held = rows_held.at[:, part, :]
+        legs.append((rows_in.at[:, part, :], held, rows_out.at[:, part, :]))
+    legs.append((vec_in, vec_held, vec_out))
+    ins = [pltpu.make_async_copy(a, b, sems_in.at[i]) for i, (a, b, c) in enumerate(legs)]
+    outs = [pltpu.make_async_copy(b, c, sems_out.at[i]) for i, (a, b, c) in enumerate(legs)]
+    for copy in ins:
+        copy.start()
+    for arrive, leave in zip(ins, outs):
+        arrive.wait()
+        leave.start()
+    for copy in outs:
+        copy.wait()
 
 
 def two_chips(queries, keys, values, lengths):
@@ -396,7 +416,7 @@
     bf, f32 = jnp.bfloat16, jnp.float32
     dma = pltpu.SemaphoreType.DMA
     hbm = pl.BlockSpec(memory_space=pl.ANY)
-    return pl.pallas_call(
+    attended, vectors = pl.pallas_call(
         pair_kernel,
         out_shape=(
             jax.ShapeDtypeStruct(queries.shape, bf),
@@ -435,6 +455,22 @@
             transcendentals=2 * heads * rows * rows,
         ),
     )(lengths, queries, keys, values)
+    return pl.pallas_call(
+        hand_over,
+        out_shape=(
+            jax.ShapeDtypeStruct(attended.shape, bf),
+            jax.ShapeDtypeStruct(vectors.shape, f32),
+        ),
+        in_specs=[hbm, hbm],
+        out_specs=(hbm, hbm),
+        scratch_shapes=[
+            pltpu.VMEM(attended.shape, bf),
+            pltpu.VMEM(vectors.shape, f32),
+            dma((SHARES + 1,)),
+            dma((SHARES + 1,)),
+        ],
+        cost_estimate=pl.CostEstimate(flops=0, bytes_accessed=4 * tok * width, transcendentals=0),
+    )(attended, vectors)
 
 
 def per_device(queries, keys, values, lengths):

time: 40.5 us -> 39.6 us (0.978)
  local copies, waits for them, and re-layouts: 2.97 us -> 0 us
  Pallas kernels: 36.8 us -> 38.8 us
    unnamed x4 -> x0, local copies, waits for them, and re-layouts: 2.97 us -> none
    pallas_call x0 -> x1, Pallas kernels: none -> 2.01 us  [two_chips(): pl.pallas_call(hand_over, out_shape=(jax.ShapeDtypeStruct(attended.shape,...]
where the time goes in v3:
time: 39.6 us; the launch traced here: 39.4 us
  Pallas kernels  38.8 us (98%)
  between operations  0.64 us (2%)
    pallas_call x1, Pallas kernels, two_chips(): pl.pallas_call(pair_kernel, out_shape=(jax.ShapeDtypeStruct(queries.shape...  36.8 us
    pallas_call x1, Pallas kernels, two_chips(): pl.pallas_call(hand_over, out_shape=(jax.ShapeDtypeStruct(attended.shape,...  2.01 us

profile of v3, /device:TPU:0, one launch (start us, length us, event | category | flops | bytes accessed | tf_op | source)
XLA Modules:
  0.0 39.4 jit_solution(15589636928407974605)
XLA Ops:
  0.6 36.8 %shard_map.59 = (bf16[1,256,2048]{2,1,0:T(8,128)(2,1)}, f32[1,8,2048]{2,1,0:T(8,128)}) custom-call(s32[1,8]{1,0:T(1,128)} %lens_hbm.1, bf16[1,256,2048]{2,1,0:T(8,128)(2,1)} %q_hbm.1, bf16[1,256,2048]{2,1,0:T(8,128)(2,1)} %k_hbm.1, bf16[1,256,2048]{2,1,0:T(8,128)(2,1)} %v_hbm.1), custom_call_target="tpu_custom_call" | custom-call | flops 2147483648 | bytes 4194304 | tf_op jit(solution)/shard_map/pallas_call | solution.py:419
  37.4 2.0 %shard_map.60 = (bf16[1,256,2048]{2,1,0:T(8,128)(2,1)}, f32[1,8,2048]{2,1,0:T(8,128)}) custom-call(bf16[1,256,2048]{2,1,0:T(8,128)(2,1)} %get-tuple-element.4.rows_in, f32[1,8,2048]{2,1,0:T(8,128)} %get-tuple-element.5.vec_in), custom_call_target="tpu_custom_call" | custom-call | bytes 2097152 | tf_op jit(solution)/shard_map/pallas_call | solution.py:458
